TPU v7x, 32 devices: a whole 2x2x4 slice. The times are simulated.
32 devices in a mesh: row: 8 (over z, core), col: 4 (over y, x).
Axes of the slice: x: 2, y: 2, z: 4, core: 2. Of those that a mesh axis runs over, the one named last changes fastest.
Arguments:
- source: bfloat16 [8192, 256], P(('row', 'col')), may hold values from -1.5 to 1.5
- target: bfloat16 [8192, 256], P(('col', 'row')), may hold values from -1.5 to 1.5
- g_init: float32 [8192], P('col'), may hold values from -25 to 25
- pairs: int32 [16, 16], P('row', 'col'), may hold values from 0 to 1, as said below
Outputs:
- f_out: float32 [8192], P('row')
- g_out: float32 [8192], P('col')
Inputs may be any that keep to these rules, and one draw needn't show every extreme that they name: Values are 0 or 1; every block of source cells and every block of target cells has at least one kept pair; the share of kept pairs differs between devices' tiles.
All inputs are finite; a program needn't handle non-finite values.
Results may differ from a plain program's by a relative error of at most 0.0003.
Values may be sent and summed in bfloat16 or wider, within the bound.
A program may use at most 64 MiB of HBM per device.

v0:
```python
import functools
import math

import jax
import jax.numpy as jnp
from jax import lax
from jax.experimental import pallas as pl
from jax.experimental.pallas import tpu as pltpu
from jax.sharding import PartitionSpec as P

EPSILON = 0.1
SCALE = math.log2(math.e) / EPSILON
UNSCALE = EPSILON * math.log(2.0)
VERY_LOW = -1e30
LANES = 128
MESH = pl.DeviceIdType.MESH


def dot_t(left, right):
    return lax.dot_general(
        left, right, (((1,), (1,)), ((), ())), preferred_element_type=jnp.float32
    )


def half_norms(cells):
    wide = cells.astype(jnp.float32)
    square = wide * wide
    high = square.astype(jnp.bfloat16)
    low = (square - high.astype(jnp.float32)).astype(jnp.bfloat16)
    ones = jnp.full((16, cells.shape[1]), 0.5, jnp.bfloat16)
    return (dot_t(ones, high) + dot_t(ones, low))[0:1, :]


def log_sum(parts):
    peak = functools.reduce(jnp.maximum, parts)
    total = functools.reduce(jnp.add, [jnp.exp2(part - peak) for part in parts])
    return peak + jnp.log2(total)


def kernel(
    n_row, n_col, blk, log2_nt, log2_ratio,
    pairs_ref, source_ref, target_ref, g_ref,
    f_ref, g_out_ref,
    sources, targets, scores, peaks, totals, shift, row_parts, col_parts,
    s_send, s_recv, t_send, t_recv, r_send, r_recv, c_send, c_recv,
):
    row, col = lax.axis_index("row"), lax.axis_index("col")
    depth = n_row // 2
    z, core = lax.div(row, 2), lax.rem(row, 2)
    rs, rt = source_ref.shape[0], target_ref.shape[0]
    n_src, n_tgt = sources.shape[0], targets.shape[0]
    width = 2 * rt

    def col_peer(step):
        return lax.rem(col + step, n_col)

    def row_peer(step):
        return lax.rem(row + step, n_row)

    def source_copy(slot, peer):
        return pltpu.make_async_remote_copy(
            src_ref=source_ref,
            dst_ref=sources.at[pl.ds(pl.multiple_of(slot * rs, rs), rs)],
            send_sem=s_send.at[peer], recv_sem=s_recv.at[slot],
            device_id={"col": peer}, device_id_type=MESH,
        )

    def target_copy(shard, way, peer, own=False):
        place = targets.at[pl.ds(pl.multiple_of(shard * rt, rt), rt)]
        return pltpu.make_async_remote_copy(
            src_ref=target_ref if own else place, dst_ref=place,
            send_sem=t_send.at[way, shard], recv_sem=t_recv.at[shard],
            device_id={"row": peer}, device_id_type=MESH,
        )

    def part_copy(parts, send, recv, slot, peer, axis):
        return pltpu.make_async_remote_copy(
            src_ref=parts.at[slot], dst_ref=parts.at[slot],
            send_sem=send.at[peer], recv_sem=recv.at[slot],
            device_id={axis: peer}, device_id_type=MESH,
        )

    sibling = 2 * z + 1 - core
    up, down = row + 2, row - 2

    barrier = pltpu.get_barrier_semaphore()
    for step in range(1, n_row):
        pl.semaphore_signal(
            barrier, inc=1, device_id={"row": row_peer(step)}, device_id_type=MESH
        )
    for step in range(1, n_col):
        pl.semaphore_signal(
            barrier, inc=1, device_id={"col": col_peer(step)}, device_id_type=MESH
        )
    sources[pl.ds(pl.multiple_of(col * rs, rs), rs), :] = source_ref[...]
    targets[pl.ds(pl.multiple_of(row * rt, rt), rt), :] = target_ref[...]
    pl.semaphore_wait(barrier, n_row + n_col - 2)

    @pl.when(z + 1 < depth)
    def _():
        target_copy(row, 0, up, True).start()

    @pl.when(z > 0)
    def _():
        target_copy(row, 1, down, True).start()

    target_copy(row, 2, sibling, True).start()
    for step in range(1, n_col):
        source_copy(col, col_peer(step)).start()

    peaks[...] = jnp.full_like(peaks, VERY_LOW)
    totals[...] = jnp.zeros_like(totals)

    def chunk(level):
        start = pl.multiple_of(level * width, width)
        cells = targets[pl.ds(start, width), :]
        base = (g_ref[:, pl.ds(start, width)] - half_norms(cells)) * SCALE
        block = lax.div(start, blk)

        def rows_step(index, _):
            at = pl.multiple_of(index * LANES, LANES)
            rows = pl.ds(at, LANES)
            kept = pairs_ref[lax.div(at, blk), block].astype(jnp.float32)
            bias = base + (1.0 - kept) * VERY_LOW
            score = dot_t(sources[rows, :], cells) * SCALE + bias
            scores[rows, pl.ds(start, width)] = score
            slices = [score[:, q : q + LANES] for q in range(0, width, LANES)]
            old = peaks[rows, :]
            peak = functools.reduce(jnp.maximum, slices, old)
            total = totals[rows, :] * jnp.exp2(old - peak)
            for part in slices:
                total += jnp.exp2(part - peak)
            peaks[rows, :] = peak
            totals[rows, :] = total
            return 0

        lax.fori_loop(0, n_src // LANES, rows_step, 0)

    for step in range(1, n_col):
        source_copy(col_peer(step), col).wait_recv()
    target_copy(sibling, 2, sibling).wait_recv()
    chunk(z)

    def chain(step, _):
        low, high = z - step, z + step

        @pl.when(low >= 0)
        def _():
            shard = 2 * low + core
            target_copy(shard, 0, down).wait_recv()

            @pl.when(z + 1 < depth)
            def _():
                target_copy(shard, 0, up).start()

            target_copy(shard, 2, sibling).start()

        @pl.when(high < depth)
        def _():
            shard = 2 * high + core
            target_copy(shard, 1, up).wait_recv()

            @pl.when(z > 0)
            def _():
                target_copy(shard, 1, down).start()

            target_copy(shard, 2, sibling).start()

        @pl.when(low >= 0)
        def _():
            target_copy(2 * low + 1 - core, 2, sibling).wait_recv()
            chunk(low)

        @pl.when(high < depth)
        def _():
            target_copy(2 * high + 1 - core, 2, sibling).wait_recv()
            chunk(high)

        return 0

    lax.fori_loop(1, depth, chain, 0)

    for index in range(n_src // LANES):
        rows = slice(index * LANES, (index + 1) * LANES)
        peak_t = peaks[rows, :].T
        total_t = totals[rows, :].T
        peak = jnp.max(peak_t, axis=0, keepdims=True)
        total = jnp.sum(total_t * jnp.exp2(peak_t - peak), axis=0, keepdims=True)
        row_parts[col, index : index + 1, :] = peak + jnp.log2(total)
    for step in range(1, n_col):
        part_copy(row_parts, r_send, r_recv, col, col_peer(step), "col").start()
    for index in range(n_src // LANES):
        cells = sources[index * LANES : (index + 1) * LANES, :]
        f_ref[index : index + 1, :] = half_norms(cells)
    for step in range(1, n_col):
        part_copy(row_parts, r_send, r_recv, col_peer(step), col, "col").wait_recv()
    row_sum = log_sum([row_parts[slot] for slot in range(n_col)])
    f_ref[...] = f_ref[...] + UNSCALE * (log2_nt - row_sum)
    for index in range(n_src // LANES):
        wide = jnp.broadcast_to(row_sum[index : index + 1, :], (LANES, LANES))
        shift[index * LANES : (index + 1) * LANES, :] = wide.T

    group = 4 if n_tgt % (4 * LANES) == 0 else 1
    tall = 64

    def cols_step(index, _):
        start = pl.multiple_of(index * group * LANES, group * LANES)

        def shifted(step):
            rows = pl.ds(pl.multiple_of(step * tall, tall), tall)
            by = shift[rows, :]
            for q in range(group):
                part = scores[rows, pl.ds(start + q * LANES, LANES)] - by
                yield part.reshape(tall // 8, 8, LANES)

        def peak_step(step, carry):
            return tuple(
                jnp.maximum(peak, jnp.max(part, axis=0))
                for peak, part in zip(carry, shifted(step))
            )

        low = jnp.full((8, LANES), VERY_LOW * 2, jnp.float32)
        peak = lax.fori_loop(0, n_src // tall, peak_step, (low,) * group)
        peak = [jnp.max(part, axis=0, keepdims=True) for part in peak]
        wide = [jnp.broadcast_to(part, (8, LANES)) for part in peak]

        def total_step(step, carry):
            return tuple(
                total + jnp.sum(jnp.exp2(part - top[None]), axis=0)
                for total, part, top in zip(carry, shifted(step), wide)
            )

        zero = jnp.zeros((8, LANES), jnp.float32)
        total = lax.fori_loop(0, n_src // tall, total_step, (zero,) * group)
        for q in range(group):
            added = jnp.sum(total[q], axis=0, keepdims=True)
            col_parts[row, pl.ds(index * group + q, 1), :] = peak[q] + jnp.log2(added)
        return 0

    lax.fori_loop(0, n_tgt // (group * LANES), cols_step, 0)

    for step in range(1, n_row):
        part_copy(col_parts, c_send, c_recv, row, row_peer(step), "row").start()
    for step in range(1, n_row):
        part_copy(col_parts, c_send, c_recv, row_peer(step), row, "row").wait_recv()
    col_sum = log_sum([col_parts[slot] for slot in range(n_row)])
    for index in range(n_tgt // LANES):
        lanes = slice(index * LANES, (index + 1) * LANES)
        g_out_ref[index : index + 1, :] = g_ref[:, lanes] - UNSCALE * (
            col_sum[index : index + 1, :] + log2_ratio
        )

    for step in range(1, n_col):
        source_copy(col, col_peer(step)).wait_send()
        part_copy(row_parts, r_send, r_recv, col, col_peer(step), "col").wait_send()
    for step in range(1, n_row):
        part_copy(col_parts, c_send, c_recv, row, row_peer(step), "row").wait_send()
    target_copy(row, 2, sibling).wait_send()

    @pl.when(z + 1 < depth)
    def _():
        target_copy(row, 0, up).wait_send()

    @pl.when(z > 0)
    def _():
        target_copy(row, 1, down).wait_send()

    def drain(step, _):
        low, high = z - step, z + step

        @pl.when(low >= 0)
        def _():
            shard = 2 * low + core
            target_copy(shard, 2, sibling).wait_send()

            @pl.when(z + 1 < depth)
            def _():
                target_copy(shard, 0, up).wait_send()

        @pl.when(high < depth)
        def _():
            shard = 2 * high + core
            target_copy(shard, 2, sibling).wait_send()

            @pl.when(z > 0)
            def _():
                target_copy(shard, 1, down).wait_send()

        return 0

    lax.fori_loop(1, depth, drain, 0)


def local(n_row, n_col, source, target, g_init, pairs):
    rs, dims = source.shape
    rt = target.shape[0]
    n_src, n_tgt = rs * n_col, rt * n_row
    blk = n_src // pairs.shape[0]
    vmem = pl.BlockSpec(memory_space=pltpu.VMEM)
    dma = pltpu.SemaphoreType.DMA
    f_out, g_out = pl.pallas_call(
        functools.partial(
            kernel, n_row, n_col, blk,
            math.log2(n_tgt * n_col), math.log2(n_tgt * n_col) - math.log2(n_src * n_row),
        ),
        out_shape=(
            jax.ShapeDtypeStruct((n_src // LANES, LANES), jnp.float32),
            jax.ShapeDtypeStruct((n_tgt // LANES, LANES), jnp.float32),
        ),
        in_specs=[pl.BlockSpec(memory_space=pltpu.SMEM), vmem, vmem, vmem],
        out_specs=(vmem, vmem),
        scratch_shapes=[
            pltpu.VMEM((n_src, dims), jnp.bfloat16),
            pltpu.VMEM((n_tgt, dims), jnp.bfloat16),
            pltpu.VMEM((n_src, n_tgt), jnp.float32),
            pltpu.VMEM((n_src, LANES), jnp.float32),
            pltpu.VMEM((n_src, LANES), jnp.float32),
            pltpu.VMEM((n_src, LANES), jnp.float32),
            pltpu.VMEM((n_col, n_src // LANES, LANES), jnp.float32),
            pltpu.VMEM((n_row, n_tgt // LANES, LANES), jnp.float32),
            dma((n_col,)), dma((n_col,)),
            dma((3, n_row)), dma((n_row,)),
            dma((n_col,)), dma((n_col,)),
            dma((n_row,)), dma((n_row,)),
        ],
        compiler_params=pltpu.CompilerParams(
            collective_id=0, has_side_effects=True, vmem_limit_bytes=40 * 1024 * 1024
        ),
    )(pairs, source, target, g_init.reshape(1, n_tgt))
    return f_out.reshape(n_src), g_out.reshape(n_tgt)


def solution(mesh):
    return jax.shard_map(
        functools.partial(local, mesh.shape["row"], mesh.shape["col"]),
        mesh=mesh,
        in_specs=(P(("row", "col"), None), P(("col", "row"), None), P("col"), P("row", "col")),
        out_specs=(P("row"), P("col")),
        check_vma=False,
    )
```

profile of v0, /device:TPU:0, one launch (start us, length us, event | category | flops | bytes accessed | tf_op | source)
XLA Modules:
  0.0 45.9 jit_solution(15289128477600055104)
XLA Ops:
  0.6 0.0 copy-start.3
  0.6 0.7 %copy-done.3 = s32[2,4]{1,0:T(2,128)S(1)} copy-done((s32[2,4]{1,0:T(2,128)S(1)}, s32[2,4]{1,0:T(2,128)}, u32[]{:S(2)}) %copy-start.3) | copy-done | bytes 56
  1.3 0.0 copy-start
  1.3 0.9 %copy-done = bf16[256,256]{1,0:T(8,128)(2,1)S(1)} copy-done((bf16[256,256]{1,0:T(8,128)(2,1)S(1)}, bf16[256,256]{1,0:T(8,128)(2,1)}, u32[]{:S(2)}) %copy-start) | copy-done | bytes 131096
  2.2 0.0 copy-start.1
  2.2 0.9 %copy-done.1 = bf16[256,256]{1,0:T(8,128)(2,1)S(1)} copy-done((bf16[256,256]{1,0:T(8,128)(2,1)S(1)}, bf16[256,256]{1,0:T(8,128)(2,1)}, u32[]{:S(2)}) %copy-start.1) | copy-done | bytes 131096
  3.1 0.0 copy-start.2
  3.1 0.7 %copy-done.2 = f32[2048]{0:T(1024)S(1)} copy-done((f32[2048]{0:T(1024)S(1)}, f32[2048]{0:T(1024)}, u32[]{:S(2)}) %copy-start.2) | copy-done | bytes 8216
  3.8 40.9 %shard_map.59 = (f32[8,128]{1,0:T(8,128)S(1)}, f32[16,128]{1,0:T(8,128)S(1)}) custom-call(s32[2,4]{1,0:T(2,128)S(1)} %copy-done.3, bf16[256,256]{1,0:T(8,128)(2,1)S(1)} %copy-done, bf16[256,256]{1,0:T(8,128)(2,1)S(1)} %copy-done.1, f32[1,2048]{1,0:T(1,128)S(1)} %bitcast.3), custom_call_target="tpu_custom_call" | custom-call | tf_op jit(solution)/shard_map/pallas_call | solution.py:301
  44.7 0.6 %copy.8 = f32[1024]{0:T(1024)} copy(f32[1024]{0:T(1024)S(1)} %bitcast.5) | data formatting | bytes 8192
  45.3 0.6 %copy.9 = f32[2048]{0:T(1024)} copy(f32[2048]{0:T(1024)S(1)} %bitcast.4) | data formatting | bytes 16384
Async XLA Ops:
  0.6 0.7 %copy-start.3 = (s32[2,4]{1,0:T(2,128)S(1)}, s32[2,4]{1,0:T(2,128)}, u32[]{:S(2)}) copy-start(s32[2,4]{1,0:T(2,128)} %pairs_ref.1) | copy-start | bytes 100
  1.3 0.9 %copy-start = (bf16[256,256]{1,0:T(8,128)(2,1)S(1)}, bf16[256,256]{1,0:T(8,128)(2,1)}, u32[]{:S(2)}) copy-start(bf16[256,256]{1,0:T(8,128)(2,1)} %source_ref.1) | copy-start | bytes 393220
  2.2 0.9 %copy-start.1 = (bf16[256,256]{1,0:T(8,128)(2,1)S(1)}, bf16[256,256]{1,0:T(8,128)(2,1)}, u32[]{:S(2)}) copy-start(bf16[256,256]{1,0:T(8,128)(2,1)} %target_ref.1) | copy-start | bytes 393220
  3.1 0.7 %copy-start.2 = (f32[2048]{0:T(1024)S(1)}, f32[2048]{0:T(1024)}, u32[]{:S(2)}) copy-start(f32[2048]{0:T(1024)} %param.6) | copy-start | bytes 24580
where the time goes:
time: 46.1 us; the launch traced here: 45.9 us
  Pallas kernels  40.9 us (89%)
  local copies, waits for them, and re-layouts  4.37 us (9%)
  between operations  0.65 us (1%)
    pallas_call x1, Pallas kernels, local(): pl.pallas_call(functools.partial(kernel, n_row, n_col, blk, math.log2(n_t...  40.9 us
    unnamed x10, local copies, waits for them, and re-layouts  4.37 us

commit v1 on v0

--- a/solution.py
+++ b/solution.py
@@ -13,6 +13,7 @@
 UNSCALE = EPSILON * math.log(2.0)
 VERY_LOW = -1e30
 LANES = 128
+PIECES = 2
 MESH = pl.DeviceIdType.MESH
 
 
@@ -39,10 +40,10 @@
 
 def kernel(
     n_row, n_col, blk, log2_nt, log2_ratio,
-    pairs_ref, source_ref, target_ref, g_ref,
+    pairs_hbm, source_ref, target_ref, g_hbm,
     f_ref, g_out_ref,
-    sources, targets, scores, peaks, totals, shift, row_parts, col_parts,
-    s_send, s_recv, t_send, t_recv, r_send, r_recv, c_send, c_recv,
+    pairs_ref, g_ref, sources, targets, scores, peaks, totals, shift, row_parts, col_parts,
+    own_sem, s_send, s_recv, t_send, t_recv, r_send, r_recv, c_send, c_recv,
 ):
     row, col = lax.axis_index("row"), lax.axis_index("col")
     depth = n_row // 2
@@ -65,11 +66,14 @@
             device_id={"col": peer}, device_id_type=MESH,
         )
 
-    def target_copy(shard, way, peer, own=False):
-        place = targets.at[pl.ds(pl.multiple_of(shard * rt, rt), rt)]
+    size = rt // PIECES
+
+    def target_copy(shard, piece, way, peer, own=False):
+        place = targets.at[pl.ds(pl.multiple_of(shard * rt + piece * size, size), size)]
         return pltpu.make_async_remote_copy(
-            src_ref=target_ref if own else place, dst_ref=place,
-            send_sem=t_send.at[way, shard], recv_sem=t_recv.at[shard],
+            src_ref=target_ref.at[pl.ds(piece * size, size)] if own else place,
+            dst_ref=place,
+            send_sem=t_send.at[way, shard, piece], recv_sem=t_recv.at[shard, piece],
             device_id={"row": peer}, device_id_type=MESH,
         )
 
@@ -92,39 +96,55 @@
         pl.semaphore_signal(
             barrier, inc=1, device_id={"col": col_peer(step)}, device_id_type=MESH
         )
-    sources[pl.ds(pl.multiple_of(col * rs, rs), rs), :] = source_ref[...]
-    targets[pl.ds(pl.multiple_of(row * rt, rt), rt), :] = target_ref[...]
+    own_copies = [
+        pltpu.make_async_copy(src, dst, own_sem.at[index])
+        for index, (src, dst) in enumerate((
+            (source_ref, sources.at[pl.ds(pl.multiple_of(col * rs, rs), rs)]),
+            (target_ref, targets.at[pl.ds(pl.multiple_of(row * rt, rt), rt)]),
+            (g_hbm, g_ref),
+            (pairs_hbm, pairs_ref),
+        ))
+    ]
+    for copy in own_copies:
+        copy.start()
     pl.semaphore_wait(barrier, n_row + n_col - 2)
 
-    @pl.when(z + 1 < depth)
-    def _():
-        target_copy(row, 0, up, True).start()
-
-    @pl.when(z > 0)
-    def _():
-        target_copy(row, 1, down, True).start()
-
-    target_copy(row, 2, sibling, True).start()
+    for piece in range(PIECES):
+
+        @pl.when(z + 1 < depth)
+        def _():
+            target_copy(row, piece, 0, up, True).start()
+
+        @pl.when(z > 0)
+        def _():
+            target_copy(row, piece, 1, down, True).start()
+
     for step in range(1, n_col):
         source_copy(col, col_peer(step)).start()
+    for piece in range(PIECES):
+        target_copy(row, piece, 2, sibling, True).start()
 
     peaks[...] = jnp.full_like(peaks, VERY_LOW)
     totals[...] = jnp.zeros_like(totals)
 
-    def chunk(level):
-        start = pl.multiple_of(level * width, width)
+    def chunk(at):
+        start = pl.multiple_of(at * width, width)
         cells = targets[pl.ds(start, width), :]
         base = (g_ref[:, pl.ds(start, width)] - half_norms(cells)) * SCALE
         block = lax.div(start, blk)
 
+        for top in range(0, n_src, blk):
+            kept = pairs_ref[top // blk, block].astype(jnp.float32)
+            bias = base + (1.0 - kept) * VERY_LOW
+            scores[top : top + blk, pl.ds(start, width)] = (
+                dot_t(sources[top : top + blk, :], cells) * SCALE + bias
+            )
+
         def rows_step(index, _):
-            at = pl.multiple_of(index * LANES, LANES)
-            rows = pl.ds(at, LANES)
-            kept = pairs_ref[lax.div(at, blk), block].astype(jnp.float32)
-            bias = base + (1.0 - kept) * VERY_LOW
-            score = dot_t(sources[rows, :], cells) * SCALE + bias
-            scores[rows, pl.ds(start, width)] = score
-            slices = [score[:, q : q + LANES] for q in range(0, width, LANES)]
+            rows = pl.ds(pl.multiple_of(index * 64, 64), 64)
+            slices = [
+                scores[rows, pl.ds(start + q, LANES)] for q in range(0, width, LANES)
+            ]
             old = peaks[rows, :]
             peak = functools.reduce(jnp.maximum, slices, old)
             total = totals[rows, :] * jnp.exp2(old - peak)
@@ -134,51 +154,63 @@
             totals[rows, :] = total
             return 0
 
-        lax.fori_loop(0, n_src // LANES, rows_step, 0)
-
+        lax.fori_loop(0, n_src // 64, rows_step, 0)
+
+    def forward(step, _):
+        low, high = z - step, z + step
+        for piece in range(PIECES):
+
+            @pl.when(low >= 0)
+            def _():
+                shard = 2 * low + core
+                target_copy(shard, piece, 0, down).wait_recv()
+
+                @pl.when(z + 1 < depth)
+                def _():
+                    target_copy(shard, piece, 0, up).start()
+
+                target_copy(shard, piece, 2, sibling).start()
+
+            @pl.when(high < depth)
+            def _():
+                shard = 2 * high + core
+                target_copy(shard, piece, 1, up).wait_recv()
+
+                @pl.when(z > 0)
+                def _():
+                    target_copy(shard, piece, 1, down).start()
+
+                target_copy(shard, piece, 2, sibling).start()
+
+        return 0
+
+    def level(at):
+        for piece in range(PIECES):
+            target_copy(2 * at + 1 - core, piece, 2, sibling).wait_recv()
+        chunk(at)
+
+    def levels(step, _):
+        low, high = z - step, z + step
+
+        @pl.when(low >= 0)
+        def _():
+            level(low)
+
+        @pl.when(high < depth)
+        def _():
+            level(high)
+
+        return 0
+
+    lax.fori_loop(1, depth - 1, forward, 0)
+    for copy in own_copies:
+        copy.wait()
     for step in range(1, n_col):
         source_copy(col_peer(step), col).wait_recv()
-    target_copy(sibling, 2, sibling).wait_recv()
-    chunk(z)
-
-    def chain(step, _):
-        low, high = z - step, z + step
-
-        @pl.when(low >= 0)
-        def _():
-            shard = 2 * low + core
-            target_copy(shard, 0, down).wait_recv()
-
-            @pl.when(z + 1 < depth)
-            def _():
-                target_copy(shard, 0, up).start()
-
-            target_copy(shard, 2, sibling).start()
-
-        @pl.when(high < depth)
-        def _():
-            shard = 2 * high + core
-            target_copy(shard, 1, up).wait_recv()
-
-            @pl.when(z > 0)
-            def _():
-                target_copy(shard, 1, down).start()
-
-            target_copy(shard, 2, sibling).start()
-
-        @pl.when(low >= 0)
-        def _():
-            target_copy(2 * low + 1 - core, 2, sibling).wait_recv()
-            chunk(low)
-
-        @pl.when(high < depth)
-        def _():
-            target_copy(2 * high + 1 - core, 2, sibling).wait_recv()
-            chunk(high)
-
-        return 0
-
-    lax.fori_loop(1, depth, chain, 0)
+    level(z)
+    lax.fori_loop(1, depth - 1, levels, 0)
+    forward(depth - 1, 0)
+    levels(depth - 1, 0)
 
     for index in range(n_src // LANES):
         rows = slice(index * LANES, (index + 1) * LANES)
@@ -255,36 +287,38 @@
         part_copy(row_parts, r_send, r_recv, col, col_peer(step), "col").wait_send()
     for step in range(1, n_row):
         part_copy(col_parts, c_send, c_recv, row, row_peer(step), "row").wait_send()
-    target_copy(row, 2, sibling).wait_send()
-
-    @pl.when(z + 1 < depth)
-    def _():
-        target_copy(row, 0, up).wait_send()
-
-    @pl.when(z > 0)
-    def _():
-        target_copy(row, 1, down).wait_send()
+    for piece in range(PIECES):
+        target_copy(row, piece, 2, sibling, True).wait_send()
+
+        @pl.when(z + 1 < depth)
+        def _():
+            target_copy(row, piece, 0, up, True).wait_send()
+
+        @pl.when(z > 0)
+        def _():
+            target_copy(row, piece, 1, down, True).wait_send()
 
     def drain(step, _):
         low, high = z - step, z + step
-
-        @pl.when(low >= 0)
-        def _():
-            shard = 2 * low + core
-            target_copy(shard, 2, sibling).wait_send()
-
-            @pl.when(z + 1 < depth)
+        for piece in range(PIECES):
+
+            @pl.when(low >= 0)
             def _():
-                target_copy(shard, 0, up).wait_send()
-
-        @pl.when(high < depth)
-        def _():
-            shard = 2 * high + core
-            target_copy(shard, 2, sibling).wait_send()
-
-            @pl.when(z > 0)
+                shard = 2 * low + core
+                target_copy(shard, piece, 2, sibling).wait_send()
+
+                @pl.when(z + 1 < depth)
+                def _():
+                    target_copy(shard, piece, 0, up).wait_send()
+
+            @pl.when(high < depth)
             def _():
-                target_copy(shard, 1, down).wait_send()
+                shard = 2 * high + core
+                target_copy(shard, piece, 2, sibling).wait_send()
+
+                @pl.when(z > 0)
+                def _():
+                    target_copy(shard, piece, 1, down).wait_send()
 
         return 0
 
@@ -307,9 +341,11 @@
             jax.ShapeDtypeStruct((n_src // LANES, LANES), jnp.float32),
             jax.ShapeDtypeStruct((n_tgt // LANES, LANES), jnp.float32),
         ),
-        in_specs=[pl.BlockSpec(memory_space=pltpu.SMEM), vmem, vmem, vmem],
+        in_specs=[pl.BlockSpec(memory_space=pltpu.HBM)] * 4,
         out_specs=(vmem, vmem),
         scratch_shapes=[
+            pltpu.SMEM(pairs.shape, jnp.int32),
+            pltpu.VMEM((1, n_tgt), jnp.float32),
             pltpu.VMEM((n_src, dims), jnp.bfloat16),
             pltpu.VMEM((n_tgt, dims), jnp.bfloat16),
             pltpu.VMEM((n_src, n_tgt), jnp.float32),
@@ -318,13 +354,14 @@
             pltpu.VMEM((n_src, LANES), jnp.float32),
             pltpu.VMEM((n_col, n_src // LANES, LANES), jnp.float32),
             pltpu.VMEM((n_row, n_tgt // LANES, LANES), jnp.float32),
+            dma((4,)),
             dma((n_col,)), dma((n_col,)),
-            dma((3, n_row)), dma((n_row,)),
+            dma((3, n_row, PIECES)), dma((n_row, PIECES)),
             dma((n_col,)), dma((n_col,)),
             dma((n_row,)), dma((n_row,)),
         ],
         compiler_params=pltpu.CompilerParams(
-            collective_id=0, has_side_effects=True, vmem_limit_bytes=40 * 1024 * 1024
+            collective_id=0, has_side_effects=True, vmem_limit_bytes=64 * 1024 * 1024
         ),
     )(pairs, source, target, g_init.reshape(1, n_tgt))
     return f_out.reshape(n_src), g_out.reshape(n_tgt)

time: 46.1 us -> 35.7 us (0.77)
  Pallas kernels: 40.9 us -> 33 us
  local copies, waits for them, and re-layouts: 4.37 us -> 1.88 us
    pallas_call x1, Pallas kernels: 40.9 us -> 33 us  [local(): pl.pallas_call(functools.partial(kernel, n_row, n_col, blk, math.log2(n_t...]
    unnamed x10 -> x4, local copies, waits for them, and re-layouts: 4.37 us -> 1.88 us
where the time goes in v1:
time: 35.7 us; the launch traced here: 35.5 us
  Pallas kernels  33 us (92%)
  local copies, waits for them, and re-layouts  1.88 us (5%)
  between operations  0.65 us (2%)
    pallas_call x1, Pallas kernels, local(): pl.pallas_call(functools.partial(kernel, n_row, n_col, blk, math.log2(n_t...  33 us
    unnamed x4, local copies, waits for them, and re-layouts  1.88 us

profile of v1, /device:TPU:0, one launch (start us, length us, event | category | flops | bytes accessed | tf_op | source)
XLA Modules:
  0.0 35.5 jit_solution(8585256023078625832)
XLA Ops:
  0.6 33.0 %shard_map.59 = (f32[8,128]{1,0:T(8,128)}, f32[16,128]{1,0:T(8,128)}) custom-call(s32[2,4]{1,0:T(2,128)} %pairs_hbm.1, bf16[256,256]{1,0:T(8,128)(2,1)} %source_ref.1, bf16[256,256]{1,0:T(8,128)(2,1)} %target_ref.1, f32[1,2048]{1,0:T(1,128)} %bitcast.3), custom_call_target="tpu_custom_call" | custom-call | tf_op jit(solution)/shard_map/pallas_call | solution.py:335
  33.7 0.0 copy-start
  33.7 1.3 %copy.8 = f32[1024]{0:T(1024)} copy(f32[1024]{0:T(1024)} %bitcast.5) | data formatting | bytes 8192
  34.9 0.0 copy-done
  34.9 0.6 %copy.9 = f32[2048]{0:T(1024)} copy(f32[2048]{0:T(1024)S(1)} %bitcast.4) | data formatting | bytes 16384
Async XLA Ops:
  33.7 1.3 %copy-start = (f32[16,128]{1,0:T(8,128)S(1)}, f32[16,128]{1,0:T(8,128)}, u32[]{:S(2)}) copy-start(f32[16,128]{1,0:T(8,128)} %get-tuple-element.5) | copy-start | bytes 24580

commit v2 on v1

--- a/solution.py
+++ b/solution.py
@@ -84,6 +84,13 @@
             device_id={axis: peer}, device_id_type=MESH,
         )
 
+    def row_copy(band, slot, peer):
+        return pltpu.make_async_remote_copy(
+            src_ref=row_parts.at[band, slot], dst_ref=row_parts.at[band, slot],
+            send_sem=r_send.at[band, peer], recv_sem=r_recv.at[band, slot],
+            device_id={"col": peer}, device_id_type=MESH,
+        )
+
     sibling = 2 * z + 1 - core
     up, down = row + 2, row - 2
 
@@ -127,13 +134,16 @@
     peaks[...] = jnp.full_like(peaks, VERY_LOW)
     totals[...] = jnp.zeros_like(totals)
 
-    def chunk(at):
+    bands = range(0, n_src, blk)
+    per = blk // LANES
+
+    def chunk(at, tops):
         start = pl.multiple_of(at * width, width)
         cells = targets[pl.ds(start, width), :]
         base = (g_ref[:, pl.ds(start, width)] - half_norms(cells)) * SCALE
         block = lax.div(start, blk)
 
-        for top in range(0, n_src, blk):
+        for top in tops:
             kept = pairs_ref[top // blk, block].astype(jnp.float32)
             bias = base + (1.0 - kept) * VERY_LOW
             scores[top : top + blk, pl.ds(start, width)] = (
@@ -154,7 +164,7 @@
             totals[rows, :] = total
             return 0
 
-        lax.fori_loop(0, n_src // 64, rows_step, 0)
+        lax.fori_loop(tops[0] // 64, (tops[-1] + blk) // 64, rows_step, 0)
 
     def forward(step, _):
         low, high = z - step, z + step
@@ -184,21 +194,22 @@
 
         return 0
 
-    def level(at):
-        for piece in range(PIECES):
-            target_copy(2 * at + 1 - core, piece, 2, sibling).wait_recv()
-        chunk(at)
-
-    def levels(step, _):
+    def level(at, tops=bands):
+        if tops[0] == 0:
+            for piece in range(PIECES):
+                target_copy(2 * at + 1 - core, piece, 2, sibling).wait_recv()
+        chunk(at, tops)
+
+    def levels(step, _, tops=bands):
         low, high = z - step, z + step
 
         @pl.when(low >= 0)
         def _():
-            level(low)
+            level(low, tops)
 
         @pl.when(high < depth)
         def _():
-            level(high)
+            level(high, tops)
 
         return 0
 
@@ -210,36 +221,40 @@
     level(z)
     lax.fori_loop(1, depth - 1, levels, 0)
     forward(depth - 1, 0)
-    levels(depth - 1, 0)
-
-    for index in range(n_src // LANES):
-        rows = slice(index * LANES, (index + 1) * LANES)
-        peak_t = peaks[rows, :].T
-        total_t = totals[rows, :].T
-        peak = jnp.max(peak_t, axis=0, keepdims=True)
-        total = jnp.sum(total_t * jnp.exp2(peak_t - peak), axis=0, keepdims=True)
-        row_parts[col, index : index + 1, :] = peak + jnp.log2(total)
-    for step in range(1, n_col):
-        part_copy(row_parts, r_send, r_recv, col, col_peer(step), "col").start()
+    for band, top in enumerate(bands):
+        levels(depth - 1, 0, range(top, top + blk, blk))
+        for index in range(per):
+            rows = slice(top + index * LANES, top + (index + 1) * LANES)
+            peak_t = peaks[rows, :].T
+            total_t = totals[rows, :].T
+            peak = jnp.max(peak_t, axis=0, keepdims=True)
+            total = jnp.sum(total_t * jnp.exp2(peak_t - peak), axis=0, keepdims=True)
+            row_parts[band, col, index : index + 1, :] = peak + jnp.log2(total)
+        for step in range(1, n_col):
+            row_copy(band, col, col_peer(step)).start()
     for index in range(n_src // LANES):
         cells = sources[index * LANES : (index + 1) * LANES, :]
         f_ref[index : index + 1, :] = half_norms(cells)
-    for step in range(1, n_col):
-        part_copy(row_parts, r_send, r_recv, col_peer(step), col, "col").wait_recv()
-    row_sum = log_sum([row_parts[slot] for slot in range(n_col)])
-    f_ref[...] = f_ref[...] + UNSCALE * (log2_nt - row_sum)
-    for index in range(n_src // LANES):
-        wide = jnp.broadcast_to(row_sum[index : index + 1, :], (LANES, LANES))
-        shift[index * LANES : (index + 1) * LANES, :] = wide.T
+
+    def finish_rows(band):
+        for step in range(1, n_col):
+            row_copy(band, col_peer(step), col).wait_recv()
+        row_sum = log_sum([row_parts[band, slot] for slot in range(n_col)])
+        lines = slice(band * per, (band + 1) * per)
+        f_ref[lines, :] = f_ref[lines, :] + UNSCALE * (log2_nt - row_sum)
+        for index in range(per):
+            wide = jnp.broadcast_to(row_sum[index : index + 1, :], (LANES, LANES))
+            at = band * blk + index * LANES
+            shift[at : at + LANES, :] = wide.T
 
     group = 4 if n_tgt % (4 * LANES) == 0 else 1
-    tall = 64
-
-    def cols_step(index, _):
+    tall = 256
+
+    def cols_step(band, index, _):
         start = pl.multiple_of(index * group * LANES, group * LANES)
 
         def shifted(step):
-            rows = pl.ds(pl.multiple_of(step * tall, tall), tall)
+            rows = pl.ds(pl.multiple_of(band * blk + step * tall, tall), tall)
             by = shift[rows, :]
             for q in range(group):
                 part = scores[rows, pl.ds(start + q * LANES, LANES)] - by
@@ -252,7 +267,7 @@
             )
 
         low = jnp.full((8, LANES), VERY_LOW * 2, jnp.float32)
-        peak = lax.fori_loop(0, n_src // tall, peak_step, (low,) * group)
+        peak = lax.fori_loop(0, blk // tall, peak_step, (low,) * group)
         peak = [jnp.max(part, axis=0, keepdims=True) for part in peak]
         wide = [jnp.broadcast_to(part, (8, LANES)) for part in peak]
 
@@ -263,13 +278,19 @@
             )
 
         zero = jnp.zeros((8, LANES), jnp.float32)
-        total = lax.fori_loop(0, n_src // tall, total_step, (zero,) * group)
+        total = lax.fori_loop(0, blk // tall, total_step, (zero,) * group)
         for q in range(group):
             added = jnp.sum(total[q], axis=0, keepdims=True)
-            col_parts[row, pl.ds(index * group + q, 1), :] = peak[q] + jnp.log2(added)
+            here = peak[q] + jnp.log2(added)
+            line = pl.ds(index * group + q, 1)
+            if band:
+                here = log_sum([col_parts[row, line, :], here])
+            col_parts[row, line, :] = here
         return 0
 
-    lax.fori_loop(0, n_tgt // (group * LANES), cols_step, 0)
+    for band in range(len(bands)):
+        finish_rows(band)
+        lax.fori_loop(0, n_tgt // (group * LANES), functools.partial(cols_step, band), 0)
 
     for step in range(1, n_row):
         part_copy(col_parts, c_send, c_recv, row, row_peer(step), "row").start()
@@ -284,7 +305,8 @@
 
     for step in range(1, n_col):
         source_copy(col, col_peer(step)).wait_send()
-        part_copy(row_parts, r_send, r_recv, col, col_peer(step), "col").wait_send()
+        for band in range(len(bands)):
+            row_copy(band, col, col_peer(step)).wait_send()
     for step in range(1, n_row):
         part_copy(col_parts, c_send, c_recv, row, row_peer(step), "row").wait_send()
     for piece in range(PIECES):
@@ -352,12 +374,12 @@
             pltpu.VMEM((n_src, LANES), jnp.float32),
             pltpu.VMEM((n_src, LANES), jnp.float32),
             pltpu.VMEM((n_src, LANES), jnp.float32),
-            pltpu.VMEM((n_col, n_src // LANES, LANES), jnp.float32),
+            pltpu.VMEM((n_src // blk, n_col, blk // LANES, LANES), jnp.float32),
             pltpu.VMEM((n_row, n_tgt // LANES, LANES), jnp.float32),
             dma((4,)),
             dma((n_col,)), dma((n_col,)),
             dma((3, n_row, PIECES)), dma((n_row, PIECES)),
-            dma((n_col,)), dma((n_col,)),
+            dma((n_src // blk, n_col)), dma((n_src // blk, n_col)),
             dma((n_row,)), dma((n_row,)),
         ],
         compiler_params=pltpu.CompilerParams(

time: 35.7 us -> 34.5 us (0.966)
  Pallas kernels: 33 us -> 31.8 us
    pallas_call x1, Pallas kernels: 33 us -> 31.8 us  [local(): pl.pallas_call(functools.partial(kernel, n_row, n_col, blk, math.log2(n_t...]
where the time goes in v2:
time: 34.5 us; the launch traced here: 34.3 us
  Pallas kernels  31.8 us (92%)
  local copies, waits for them, and re-layouts  1.88 us (5%)
  between operations  0.65 us (2%)
    pallas_call x1, Pallas kernels, local(): pl.pallas_call(functools.partial(kernel, n_row, n_col, blk, math.log2(n_t...  31.8 us
    unnamed x4, local copies, waits for them, and re-layouts  1.88 us

profile of v2, /device:TPU:0, one launch (start us, length us, event | category | flops | bytes accessed | tf_op | source)
XLA Modules:
  0.0 34.3 jit_solution(8450669125947492867)
XLA Ops:
  0.6 31.8 %shard_map.59 = (f32[8,128]{1,0:T(8,128)}, f32[16,128]{1,0:T(8,128)}) custom-call(s32[2,4]{1,0:T(2,128)} %pairs_hbm.1, bf16[256,256]{1,0:T(8,128)(2,1)} %source_ref.1, bf16[256,256]{1,0:T(8,128)(2,1)} %target_ref.1, f32[1,2048]{1,0:T(1,128)} %bitcast.3), custom_call_target="tpu_custom_call" | custom-call | tf_op jit(solution)/shard_map/pallas_call | solution.py:357
  32.4 0.0 copy-start
  32.4 1.3 %copy.8 = f32[1024]{0:T(1024)} copy(f32[1024]{0:T(1024)} %bitcast.5) | data formatting | bytes 8192
  33.7 0.0 copy-done
  33.7 0.6 %copy.9 = f32[2048]{0:T(1024)} copy(f32[2048]{0:T(1024)S(1)} %bitcast.4) | data formatting | bytes 16384
Async XLA Ops:
  32.4 1.3 %copy-start = (f32[16,128]{1,0:T(8,128)S(1)}, f32[16,128]{1,0:T(8,128)}, u32[]{:S(2)}) copy-start(f32[16,128]{1,0:T(8,128)} %get-tuple-element.5) | copy-start | bytes 24580

commit v3 on v2

--- a/solution.py
+++ b/solution.py
@@ -151,7 +151,7 @@
             )
 
         def rows_step(index, _):
-            rows = pl.ds(pl.multiple_of(index * 64, 64), 64)
+            rows = pl.ds(pl.multiple_of(index * LANES, LANES), LANES)
             slices = [
                 scores[rows, pl.ds(start + q, LANES)] for q in range(0, width, LANES)
             ]
@@ -164,7 +164,7 @@
             totals[rows, :] = total
             return 0
 
-        lax.fori_loop(tops[0] // 64, (tops[-1] + blk) // 64, rows_step, 0)
+        lax.fori_loop(tops[0] // LANES, (tops[-1] + blk) // LANES, rows_step, 0)
 
     def forward(step, _):
         low, high = z - step, z + step
@@ -248,7 +248,7 @@
             shift[at : at + LANES, :] = wide.T
 
     group = 4 if n_tgt % (4 * LANES) == 0 else 1
-    tall = 256
+    tall = blk
 
     def cols_step(band, index, _):
         start = pl.multiple_of(index * group * LANES, group * LANES)

time: 34.5 us -> 33.9 us (0.983)
  Pallas kernels: 31.8 us -> 31.2 us
    pallas_call x1, Pallas kernels: 31.8 us -> 31.2 us  [local(): pl.pallas_call(functools.partial(kernel, n_row, n_col, blk, math.log2(n_t...]
where the time goes in v3:
time: 33.9 us; the launch traced here: 33.7 us
  Pallas kernels  31.2 us (92%)
  local copies, waits for them, and re-layouts  1.88 us (6%)
  between operations  0.65 us (2%)
    pallas_call x1, Pallas kernels, local(): pl.pallas_call(functools.partial(kernel, n_row, n_col, blk, math.log2(n_t...  31.2 us
    unnamed x4, local copies, waits for them, and re-layouts  1.88 us

profile of v3, /device:TPU:0, one launch (start us, length us, event | category | flops | bytes accessed | tf_op | source)
XLA Modules:
  0.0 33.7 jit_solution(5693328478764966017)
XLA Ops:
  0.6 31.2 %shard_map.59 = (f32[8,128]{1,0:T(8,128)}, f32[16,128]{1,0:T(8,128)}) custom-call(s32[2,4]{1,0:T(2,128)} %pairs_hbm.1, bf16[256,256]{1,0:T(8,128)(2,1)} %source_ref.1, bf16[256,256]{1,0:T(8,128)(2,1)} %target_ref.1, f32[1,2048]{1,0:T(1,128)} %bitcast.3), custom_call_target="tpu_custom_call" | custom-call | tf_op jit(solution)/shard_map/pallas_call | solution.py:357
  31.8 0.0 copy-start
  31.8 1.3 %copy.8 = f32[1024]{0:T(1024)} copy(f32[1024]{0:T(1024)} %bitcast.5) | data formatting | bytes 8192
  33.1 0.0 copy-done
  33.1 0.6 %copy.9 = f32[2048]{0:T(1024)} copy(f32[2048]{0:T(1024)S(1)} %bitcast.4) | data formatting | bytes 16384
Async XLA Ops:
  31.8 1.3 %copy-start = (f32[16,128]{1,0:T(8,128)S(1)}, f32[16,128]{1,0:T(8,128)}, u32[]{:S(2)}) copy-start(f32[16,128]{1,0:T(8,128)} %get-tuple-element.5) | copy-start | bytes 24580
